TPU v7x, 32 devices: a whole 2x2x4 slice. The times are simulated.
32 devices in a mesh: req: 16 (over z, y, x), tp: 2 (over core).
Axes of the slice: x: 2, y: 2, z: 4, core: 2. Of those that a mesh axis runs over, the one named last changes fastest.
Arguments:
- residual: bfloat16 [512, 2048], P('req'), may hold values from -6 to 6
- fresh_qkv: bfloat16 [512, 3, 2048], P('req', None, 'tp'), may hold values from -32 to 32
- kv_cache: bfloat16 [512, 24, 2, 2048], P('req', None, None, 'tp'), may hold values from -32 to 32
- cache_len: int32 [512], P('req'), may hold values from 2 to 24, as said below
- out_proj: bfloat16 [2048, 2048], P('tp'), may hold values from -0.125 to 0.125
- norm_gain: float32 [2048], replicated, may hold values from 0.1 to 1.9
- router_weight: float32 [2048, 16], replicated, may hold values from -7.9549513 to 7.9549513
- expert_ids: int32 [512, 8], P('req'), may hold values from 0 to 15, all different within a row; in each aligned block of 32 rows (0 to 31, 32 to 63, ...) at most 32 rows name the same one
- gate_up: bfloat16 [16, 2048, 2, 1024], P('req', None, None, 'tp'), may hold values from -0.125 to 0.125
- down_proj: bfloat16 [16, 1024, 2048], P('req', 'tp'), may hold values from -0.1875 to 0.1875
Outputs:
- layer_out: bfloat16 [512, 2048], P('req', 'tp')
Inputs may be any that keep to these rules, and one draw needn't show every extreme that they name: `expert_ids`: each row names 8 different experts; among the 32 rows of one device no expert is named by more than 32 rows, and some device reaches 32. `cache_len`: some request uses all 24 positions.
All inputs are finite; a program needn't handle non-finite values.
Results may differ from a plain program's by a relative error of at most 0.018.
Values may be sent and summed in bfloat16 or wider, within the bound.
A program may use at most 128 MiB of HBM per device.

v0:
```python
import jax
import jax.numpy as jnp
from jax import lax
from jax.sharding import PartitionSpec as P

HD = 128


def rms_normed(hidden_in, gain):
    values = hidden_in.astype(jnp.float32)
    scale_inv = lax.rsqrt(jnp.mean(values * values, axis=-1, keepdims=True) + 1e-05)
    return (values * scale_inv * gain).astype(jnp.bfloat16)


def attend(fresh_qkv, kv_cache, cache_len):
    requests, ctx_len = (kv_cache.shape[0], kv_cache.shape[1])
    local_heads = fresh_qkv.shape[2] // HD
    queries = fresh_qkv[:, 0].reshape(requests, local_heads, HD)
    new_keys = fresh_qkv[:, 1].reshape(requests, local_heads, HD)
    new_values = fresh_qkv[:, 2].reshape(requests, local_heads, HD)
    cache_keys = kv_cache[:, :, 0].reshape(requests, ctx_len, local_heads, HD)
    cache_values = kv_cache[:, :, 1].reshape(requests, ctx_len, local_heads, HD)
    factor = HD ** (-0.5)
    scores = (
        jnp.einsum("nhd,nchd->nhc", queries, cache_keys, preferred_element_type=jnp.float32)
        * factor
    )
    own_score = (
        jnp.einsum("nhd,nhd->nh", queries, new_keys, preferred_element_type=jnp.float32) * factor
    )
    valid = (jnp.arange(ctx_len, dtype=jnp.int32)[None, :] < cache_len[:, None])[:, None, :]
    masked = jnp.where(valid, scores, -jnp.inf)
    top_score = jnp.maximum(jnp.max(masked, axis=-1), own_score)
    expos = jnp.where(valid, jnp.exp(masked - top_score[..., None]), 0.0)
    own_expo = jnp.exp(own_score - top_score)
    total = jnp.sum(expos, axis=-1) + own_expo
    weights = (expos / total[..., None]).astype(jnp.bfloat16)
    own_weight = (own_expo / total).astype(jnp.bfloat16)
    mixed = jnp.einsum("nhc,nchd->nhd", weights, cache_values, preferred_element_type=jnp.float32)
    mixed = mixed + own_weight.astype(jnp.float32)[..., None] * new_values.astype(jnp.float32)
    return mixed.astype(jnp.bfloat16).reshape(requests, local_heads * HD)


def local(
    residual,
    fresh_qkv,
    kv_cache,
    cache_len,
    out_proj,
    norm_gain,
    router_weight,
    expert_ids,
    gate_up,
    down_proj,
):
    tp_place = lax.axis_index("tp")
    me = lax.axis_index("req")
    experts = lax.axis_size("req")
    attended = attend(fresh_qkv, kv_cache, cache_len)
    partial_value = jnp.dot(attended, out_proj, preferred_element_type=jnp.float32)
    summed = lax.psum(partial_value, "tp")
    hidden = (residual.astype(jnp.float32) + summed).astype(jnp.bfloat16)
    normed = rms_normed(hidden, norm_gain)
    rows = lax.all_gather(normed, "req", axis=0, tiled=True)
    logits = jnp.dot(normed.astype(jnp.float32), router_weight, precision=lax.Precision.HIGHEST)
    named = jnp.any(
        expert_ids[:, :, None] == jnp.arange(experts, dtype=jnp.int32)[None, None, :], axis=1
    )
    gates = jax.nn.softmax(jnp.where(named, logits, -jnp.inf), axis=-1)
    gates_all = lax.all_gather(gates, "req", axis=0, tiled=True)
    mine = jnp.arange(experts, dtype=jnp.int32)[None, :] == me
    weight = jnp.sum(jnp.where(mine, gates_all, 0.0), axis=1, keepdims=True)
    gate_part = jnp.dot(rows, gate_up[0, :, 0], preferred_element_type=jnp.float32)
    up_part = jnp.dot(rows, gate_up[0, :, 1], preferred_element_type=jnp.float32)
    inner = (jax.nn.silu(gate_part) * up_part).astype(jnp.bfloat16)
    result = jnp.dot(inner, down_proj[0], preferred_element_type=jnp.float32)
    own = lax.psum_scatter(result * weight, "tp", scatter_dimension=1, tiled=True)
    moe_share = lax.psum_scatter(own, "req", scatter_dimension=0, tiled=True)
    width_here = moe_share.shape[1]
    own_cols = lax.dynamic_slice_in_dim(hidden, tp_place * width_here, width_here, 1)
    return (own_cols.astype(jnp.float32) + moe_share).astype(jnp.bfloat16)


def solution(mesh):
    in_specs = (
        P("req", None),
        P("req", None, "tp"),
        P("req", None, None, "tp"),
        P("req"),
        P("tp", None),
        P(),
        P(),
        P("req", None),
        P("req", None, None, "tp"),
        P("req", "tp", None),
    )
    out_specs = P("req", "tp")
    return jax.shard_map(local, mesh=mesh, in_specs=in_specs, out_specs=out_specs, check_vma=False)
```

profile of v0, /device:TPU:0, one launch (start us, length us, event | category | flops | bytes accessed | tf_op | source)
XLA Modules:
  0.0 234.0 jit_solution(13227113264910571109)
XLA Ops:
  6.5 0.8 iota_compare_fusion.1
  7.4 0.9 convert_bitcast_fusion
  8.4 0.1 fusion.20
  8.6 17.1 %slice_reduce_fusion = (bf16[32,24,1024]{2,1,0:T(8,128)(2,1)}, bf16[32,24,1024]{2,1,0:T(8,128)(2,1)S(1)}) fusion(bf16[32,24,2,1024]{3,2,1,0:T(2,128)(2,1)} %param.12), kind=kLoop, calls=%fused_computation.1 | loop fusion | bytes 6291456 | tf_op jit(solution)/shard_map/slice | solution.py:22
  25.7 0.9 fusion.6
  26.7 0.1 copy.26
  27.0 0.2 copy.31
  27.2 2.0 fusion.3
  29.2 0.1 fusion.19
  29.3 3.8 %fusion.24 = f32[32,2048]{1,0:T(8,128)} fusion(bf16[1024,2048]{1,0:T(8,128)(2,1)} %param.14, bf16[4,8,8,128]{3,2,1,0:T(8,128)(2,1)S(1)} %bitcast.84), kind=kOutput, calls=%fused_computation.40 | convolution fusion | flops 134217728 | bytes 4521984 | tf_op jit(solution)/shard_map/dot_general | solution.py:60
  33.2 21.1 %all-reduce.2.cloned.1.call-done = f32[32,2048]{1,0:T(8,128)} async-done(((f32[32,2048]{1,0:T(8,128)}), f32[32,2048]{1,0:T(8,128)}) %all-reduce.2.cloned.1.call-update) | async-done | bytes 262160 | tf_op jit(solution)/shard_map/psum | solution.py:61
  54.3 1.1 fusion.15
  55.4 0.7 fusion.17
  56.3 10.4 %fusion.33 = (bf16[1,2048,1,512]{3,2,1,0:T(2,128)(2,1)}, bf16[1,2048,1,512]{3,2,1,0:T(2,128)(2,1)}) fusion(bf16[1,2048,2,512]{3,2,1,0:T(2,128)(2,1)} %param.18), kind=kLoop, calls=%fused_computation.61 | loop fusion | bytes 8388608 | tf_op jit(solution)/shard_map/slice | solution.py:73
  66.7 0.2 fusion.34
  67.0 41.8 %all-gather = f32[16,32,16]{1,2,0:T(8,128)S(1)} all-gather(f32[1,32,16]{1,2,0:T(8,128)S(1)} %divide_bitcast_fusion), channel_id=1, replica_groups=mesh['req'=16,'tp'=2] {'req'}, dimensions={0}, use_global_device_ids=true | all-gather | bytes 34816 | tf_op jit(solution)/shard_map/all_gather | solution.py:70
  108.9 0.1 reshape.46
  109.0 0.1 select_reduce_fusion
  109.1 10.6 %all-gather.3.cloned.1.call-done = bf16[512,2048]{1,0:T(8,128)(2,1)} async-done(((bf16[32,2048]{1,0:T(8,128)(2,1)}), bf16[512,2048]{1,0:T(8,128)(2,1)}) %all-gather.3.cloned.1.call-update) | async-done | bytes 2097168 | tf_op jit(solution)/shard_map/all_gather | solution.py:64
  119.6 4.1 %fusion.1 = f32[512,512]{1,0:T(8,128)S(1)} fusion(bf16[512,2048]{1,0:T(8,128)(2,1)} %all-gather.3.cloned.1.call-done, bf16[1,2048,1,512]{3,2,1,0:T(2,128)(2,1)} %get-tuple-element.9), kind=kOutput, calls=%fused_computation.6 | convolution fusion | flops 1073741824 | bytes 5242880 | tf_op jit(solution)/shard_map/dot_general | solution.py:73
  123.7 7.3 %convolution_multiply_fusion = f32[512,2048]{1,0:T(8,128)} fusion(bf16[1,512,2048]{2,1,0:T(8,128)(2,1)S(1)} %copy-done, f32[512]{0:T(512)S(1)} %select_reduce_fusion, bf16[512,2048]{1,0:T(8,128)(2,1)} %all-gather.3.cloned.1.call-done, bf16[1,2048,1,512]{3,2,1,0:T(2,128)(2,1)} %get-tuple-element.10, f32[512,512]{1,0:T(8,128)S(1)} %fusion.1), kind=kOutput, calls=%fused_computation | convolution fusion | flops 2150105088 | bytes 11536384 | tf_op jit(solution)/shard_map/dot_general | solution.py:76
  131.1 10.8 %reduce-scatter.3.cloned.1.call-done = f32[512,1024]{1,0:T(8,128)} async-done(((f32[512,2048]{1,0:T(8,128)}), f32[512,1024]{1,0:T(8,128)}) %reduce-scatter.3.cloned.1.call-update) | async-done | bytes 2097168 | tf_op jit(solution)/shard_map/reduce_scatter | solution.py:77
  141.9 84.1 %reduce-scatter.5.cloned.1.call-done = f32[32,1024]{1,0:T(8,128)} async-done(((f32[512,1024]{1,0:T(8,128)}), f32[32,1024]{1,0:T(8,128)}) %reduce-scatter.5.cloned.1.call-update) | async-done | bytes 131088 | tf_op jit(solution)/shard_map/reduce_scatter | solution.py:78
  226.0 1.5 add_convert_fusion.1
  (37 shorter events, 0.7 us)
Async XLA Ops:
  6.5 117.2 %copy-start = (bf16[1,512,2048]{2,1,0:T(8,128)(2,1)S(1)}, bf16[1,512,2048]{2,1,0:T(8,128)(2,1)}, u32[]{:S(2)}) copy-start(bf16[1,512,2048]{2,1,0:T(8,128)(2,1)} %param.19) | copy-start | bytes 6291460
  6.5 47.7 %all-reduce.2.cloned.1.call-start = ((), (), s32[]{:S(2)}) async-start(), calls=%async_computation.2 | async-start | bytes 524288 | tf_op jit(solution)/shard_map/psum | solution.py:61
  29.3 25.0 %copy-start.2 = (bf16[32,2048]{1,0:T(8,128)(2,1)S(1)}, bf16[32,2048]{1,0:T(8,128)(2,1)}, u32[]{:S(2)}) copy-start(bf16[32,2048]{1,0:T(8,128)(2,1)} %param.10) | copy-start | bytes 393220
  29.3 26.1 %copy-start.4 = (f32[2048]{0:T(1024)S(1)}, f32[2048]{0:T(1024)}, u32[]{:S(2)}) copy-start(f32[2048]{0:T(1024)} %param.15) | copy-start | bytes 24580
  29.3 26.9 %copy-start.5 = (s32[32,8]{0,1:T(8,128)S(1)}, s32[32,8]{0,1:T(8,128)}, u32[]{:S(2)}) copy-start(s32[32,8]{0,1:T(8,128)} %param.17) | copy-start | bytes 3076
  33.1 86.5 %all-gather.3.cloned.1.call-start = ((), (), s32[]{:S(2)}) async-start(), calls=%async_computation.3 | async-start | bytes 2228224 | tf_op jit(solution)/shard_map/all_gather | solution.py:64
  56.1 85.7 %reduce-scatter.3.cloned.1.call-start = ((), (), s32[]{:S(2)}) async-start(), calls=%async_computation.4 | async-start | bytes 6291456 | tf_op jit(solution)/shard_map/reduce_scatter | solution.py:77
  56.2 10.5 %copy-start.1 = (bf16[32,2048]{1,0:T(8,128)(2,1)S(1)}, bf16[32,2048]{1,0:T(8,128)(2,1)}, u32[]{:S(2)}) copy-start(bf16[32,2048]{1,0:T(8,128)(2,1)} %fusion.17) | copy-start | bytes 393220
  56.3 10.5 %copy-start.3 = (f32[2048,16]{0,1:T(8,128)S(1)}, f32[2048,16]{0,1:T(8,128)}, u32[]{:S(2)}) copy-start(f32[2048,16]{0,1:T(8,128)} %param.16) | copy-start | bytes 393220
  131.0 95.0 %reduce-scatter.5.cloned.1.call-start = ((), (), s32[]{:S(2)}) async-start(), calls=%async_computation.5 | async-start | bytes 2228224 | tf_op jit(solution)/shard_map/reduce_scatter | solution.py:78
Sparse Core Ops, SparseCore 0:
  33.3 20.9 all-reduce.1
  57.4 62.1 all-gather.2
  131.1 10.6 reduce-scatter.2
  144.0 81.9 reduce-scatter.4
where the time goes:
time: 234 us
  waiting for transfers between devices  127 us (54%)
  blocking collectives  41.8 us (18%)
  local copies, waits for them, and re-layouts  28.3 us (12%)
  matrix products  18.2 us (8%)
  between operations  13.3 us (6%)
  other arithmetic  5.64 us (2%)
    reduce_scatter x1, waiting for transfers between devices, local(): moe_share = lax.psum_scatter(own, 'req', scatter_dimension=0, tiled=True)  84.1 us
    all_gather x1, blocking collectives, local(): gates_all = lax.all_gather(gates, 'req', axis=0, tiled=True)  41.8 us
    psum x1, waiting for transfers between devices, local(): summed = lax.psum(partial_value, 'tp')  21.1 us
    slice x1, local copies, waits for them, and re-layouts, attend(): cache_values = kv_cache[:, :, 1].reshape(requests, ctx_len, local_heads, HD)  17.1 us
    reduce_scatter x1, waiting for transfers between devices, local(): lax.psum_scatter(result * weight, 'tp', scatter_dimension=1, tiled=True)  10.8 us
    all_gather x1, waiting for transfers between devices, local(): rows = lax.all_gather(normed, 'req', axis=0, tiled=True)  10.6 us
    slice x1, local copies, waits for them, and re-layouts, local(): gate_up[0, :, 0]  10.4 us
    dot_general x1, matrix products, local(): result = jnp.dot(inner, down_proj[0], preferred_element_type=jnp.float32)  7.25 us
  transfers between devices with their start and end apart: 4, of which 4 were waited for; matrix products, arithmetic and copies ran while one was open for 5% of the time, Pallas kernels for 0%

commit v1 on v0

--- a/solution.py
+++ b/solution.py
@@ -58,7 +58,8 @@
     experts = lax.axis_size("req")
     attended = attend(fresh_qkv, kv_cache, cache_len)
     partial_value = jnp.dot(attended, out_proj, preferred_element_type=jnp.float32)
-    summed = lax.psum(partial_value, "tp")
+    parts = lax.all_gather(partial_value, "tp", axis=0, tiled=False)
+    summed = parts.sum(axis=0)
     hidden = (residual.astype(jnp.float32) + summed).astype(jnp.bfloat16)
     normed = rms_normed(hidden, norm_gain)
     rows = lax.all_gather(normed, "req", axis=0, tiled=True)

time: 234 us -> 214 us (0.915)
  waiting for transfers between devices: 127 us -> 104 us
  blocking collectives: 41.8 us -> 45.4 us
    psum x1 -> x0, waiting for transfers between devices: 21.1 us -> none  [local(): summed = lax.psum(partial_value, 'tp')]
    all_gather x0 -> x1, blocking collectives: none -> 2.39 us  [local(): parts = lax.all_gather(partial_value, 'tp', axis=0, tiled=False)]
  transfers between devices with their start and end apart: 4 -> 3, of which waited for: 4 -> 3; matrix products, arithmetic and copies ran while one was open for 5% -> 6% of each run, Pallas kernels for 0% -> 0%
where the time goes in v1:
time: 214 us
  waiting for transfers between devices  104 us (49%)
  blocking collectives  45.4 us (21%)
  local copies, waits for them, and re-layouts  28.3 us (13%)
  matrix products  18.5 us (9%)
  between operations  13.3 us (6%)
  other arithmetic  4.72 us (2%)
    reduce_scatter x1, waiting for transfers between devices, local(): moe_share = lax.psum_scatter(own, 'req', scatter_dimension=0, tiled=True)  84.3 us
    all_gather x1, blocking collectives, local(): gates_all = lax.all_gather(gates, 'req', axis=0, tiled=True)  43 us
    slice x1, local copies, waits for them, and re-layouts, attend(): cache_values = kv_cache[:, :, 1].reshape(requests, ctx_len, local_heads, HD)  17.1 us
    reduce_scatter x1, waiting for transfers between devices, local(): lax.psum_scatter(result * weight, 'tp', scatter_dimension=1, tiled=True)  10.8 us
    slice x1, local copies, waits for them, and re-layouts, local(): gate_up[0, :, 0]  10.4 us
    all_gather x1, waiting for transfers between devices, local(): rows = lax.all_gather(normed, 'req', axis=0, tiled=True)  8.62 us
    dot_general x1, matrix products, local(): result = jnp.dot(inner, down_proj[0], preferred_element_type=jnp.float32)  7.3 us
  transfers between devices with their start and end apart: 3, of which 3 were waited for; matrix products, arithmetic and copies ran while one was open for 6% of the time, Pallas kernels for 0%

profile of v1, /device:TPU:0, one launch (start us, length us, event | category | flops | bytes accessed | tf_op | source)
XLA Modules:
  0.0 214.0 jit_solution(6440824016193036164)
XLA Ops:
  6.5 0.8 iota_compare_fusion.1
  7.4 0.9 convert_bitcast_fusion
  8.4 0.1 fusion.20
  8.6 17.1 %slice_reduce_fusion = (bf16[32,24,1024]{2,1,0:T(8,128)(2,1)}, bf16[32,24,1024]{2,1,0:T(8,128)(2,1)S(1)}) fusion(bf16[32,24,2,1024]{3,2,1,0:T(2,128)(2,1)} %param.12), kind=kLoop, calls=%fused_computation.1 | loop fusion | bytes 6291456 | tf_op jit(solution)/shard_map/slice | solution.py:22
  25.7 0.9 fusion.6
  26.7 0.1 copy.26
  27.0 0.2 copy.31
  27.2 2.0 fusion.3
  29.2 0.1 fusion.19
  29.3 3.0 %fusion.24 = f32[32,2048]{1,0:T(8,128)S(1)} fusion(bf16[1024,2048]{1,0:T(8,128)(2,1)} %param.14, bf16[4,8,8,128]{3,2,1,0:T(8,128)(2,1)S(1)} %bitcast.86), kind=kOutput, calls=%fused_computation.40 | convolution fusion | flops 134217728 | bytes 4521984 | tf_op jit(solution)/shard_map/dot_general | solution.py:60
  32.4 2.4 %all-gather = f32[64,2048]{1,0:T(8,128)S(1)} all-gather(f32[32,2048]{1,0:T(8,128)S(1)} %fusion.24), channel_id=2, replica_groups=mesh['req'=16,'tp'=2] {'tp'}, dimensions={0}, use_global_device_ids=true | all-gather | bytes 786432 | tf_op jit(solution)/shard_map/all_gather | solution.py:61
  34.8 0.2 fusion.15
  35.0 0.7 fusion.17
  35.9 1.1 fusion.34
  37.0 43.0 %all-gather.1 = f32[16,32,16]{1,2,0:T(8,128)S(1)} all-gather(f32[1,32,16]{1,2,0:T(8,128)S(1)} %divide_bitcast_fusion), channel_id=1, replica_groups=mesh['req'=16,'tp'=2] {'req'}, dimensions={0}, use_global_device_ids=true | all-gather | bytes 34816 | tf_op jit(solution)/shard_map/all_gather | solution.py:71
  80.1 0.1 reshape.47
  80.2 0.1 select_reduce_fusion
  80.3 10.4 %fusion.33 = (bf16[1,2048,1,512]{3,2,1,0:T(2,128)(2,1)}, bf16[1,2048,1,512]{3,2,1,0:T(2,128)(2,1)}) fusion(bf16[1,2048,2,512]{3,2,1,0:T(2,128)(2,1)} %param.18), kind=kLoop, calls=%fused_computation.61 | loop fusion | bytes 8388608 | tf_op jit(solution)/shard_map/slice | solution.py:74
  90.7 8.6 %all-gather.4.cloned.1.call-done = bf16[512,2048]{1,0:T(8,128)(2,1)} async-done(((bf16[32,2048]{1,0:T(8,128)(2,1)}), bf16[512,2048]{1,0:T(8,128)(2,1)}) %all-gather.4.cloned.1.call-update) | async-done | bytes 2097168 | tf_op jit(solution)/shard_map/all_gather | solution.py:65
  99.3 4.1 %fusion.1 = f32[512,512]{1,0:T(8,128)S(1)} fusion(bf16[512,2048]{1,0:T(8,128)(2,1)} %all-gather.4.cloned.1.call-done, bf16[1,2048,1,512]{3,2,1,0:T(2,128)(2,1)} %get-tuple-element.9), kind=kOutput, calls=%fused_computation.6 | convolution fusion | flops 1073741824 | bytes 5242880 | tf_op jit(solution)/shard_map/dot_general | solution.py:74
  103.4 7.3 %convolution_multiply_fusion = f32[512,2048]{1,0:T(8,128)} fusion(bf16[1,512,2048]{2,1,0:T(8,128)(2,1)S(1)} %copy-done, f32[512]{0:T(512)S(1)} %select_reduce_fusion, bf16[512,2048]{1,0:T(8,128)(2,1)} %all-gather.4.cloned.1.call-done, bf16[1,2048,1,512]{3,2,1,0:T(2,128)(2,1)} %get-tuple-element.10, f32[512,512]{1,0:T(8,128)S(1)} %fusion.1), kind=kOutput, calls=%fused_computation | convolution fusion | flops 2150105088 | bytes 11536384 | tf_op jit(solution)/shard_map/dot_general | solution.py:77
  110.8 10.8 %reduce-scatter.3.cloned.1.call-done = f32[512,1024]{1,0:T(8,128)} async-done(((f32[512,2048]{1,0:T(8,128)}), f32[512,1024]{1,0:T(8,128)}) %reduce-scatter.3.cloned.1.call-update) | async-done | bytes 2097168 | tf_op jit(solution)/shard_map/reduce_scatter | solution.py:78
  121.6 84.3 %reduce-scatter.5.cloned.1.call-done = f32[32,1024]{1,0:T(8,128)} async-done(((f32[512,1024]{1,0:T(8,128)}), f32[32,1024]{1,0:T(8,128)}) %reduce-scatter.5.cloned.1.call-update) | async-done | bytes 131088 | tf_op jit(solution)/shard_map/reduce_scatter | solution.py:79
  205.9 1.5 add_convert_fusion.1
  (34 shorter events, 0.7 us)
Async XLA Ops:
  6.5 96.9 %copy-start = (bf16[1,512,2048]{2,1,0:T(8,128)(2,1)S(1)}, bf16[1,512,2048]{2,1,0:T(8,128)(2,1)}, u32[]{:S(2)}) copy-start(bf16[1,512,2048]{2,1,0:T(8,128)(2,1)} %param.19) | copy-start | bytes 6291460
  6.5 92.8 %all-gather.4.cloned.1.call-start = ((), (), s32[]{:S(2)}) async-start(), calls=%async_computation.2 | async-start | bytes 2228224 | tf_op jit(solution)/shard_map/all_gather | solution.py:65
  29.3 5.5 %copy-start.1 = (bf16[32,2048]{1,0:T(8,128)(2,1)S(1)}, bf16[32,2048]{1,0:T(8,128)(2,1)}, u32[]{:S(2)}) copy-start(bf16[32,2048]{1,0:T(8,128)(2,1)} %param.10) | copy-start | bytes 393220
  32.4 2.6 %copy-start.3 = (f32[2048]{0:T(1024)S(1)}, f32[2048]{0:T(1024)}, u32[]{:S(2)}) copy-start(f32[2048]{0:T(1024)} %param.15) | copy-start | bytes 24580
  32.4 3.5 %copy-start.4 = (s32[32,8]{0,1:T(8,128)S(1)}, s32[32,8]{0,1:T(8,128)}, u32[]{:S(2)}) copy-start(s32[32,8]{0,1:T(8,128)} %param.17) | copy-start | bytes 3076
  32.4 3.5 %copy-start.2 = (f32[2048,16]{0,1:T(8,128)S(1)}, f32[2048,16]{0,1:T(8,128)}, u32[]{:S(2)}) copy-start(f32[2048,16]{0,1:T(8,128)} %param.16) | copy-start | bytes 393220
  35.8 85.8 %reduce-scatter.3.cloned.1.call-start = ((), (), s32[]{:S(2)}) async-start(), calls=%async_computation.3 | async-start | bytes 6291456 | tf_op jit(solution)/shard_map/reduce_scatter | solution.py:78
  110.8 95.1 %reduce-scatter.5.cloned.1.call-start = ((), (), s32[]{:S(2)}) async-start(), calls=%async_computation.4 | async-start | bytes 2228224 | tf_op jit(solution)/shard_map/reduce_scatter | solution.py:79
Sparse Core Ops, SparseCore 0:
  35.9 63.4 all-gather.3
  110.9 10.6 reduce-scatter.2
  124.0 81.8 reduce-scatter.4
